TPU v7x, 128 devices: a whole 4x4x4 slice. The times are simulated.
128 devices in a mesh: leaf: 32 (over z, y, x_lo), blk: 4 (over x_hi, core).
Axes of the slice: x: 4 (x_hi: 2, x_lo: 2; x = x_hi * 2 + x_lo), y: 4, z: 4, core: 2. Of those that a mesh axis runs over, the one named last changes fastest.
Arguments:
- noise_root: float32 [4096, 512], P('blk'), may hold values from -6 to 6
- block_root: bfloat16 [4096, 4096], P('leaf', 'blk'), as said below
- noise_first: float32 [2048, 1024], P('blk', 'leaf'), may hold values from -6 to 6
- block_first: bfloat16 [4096, 2048], P('leaf', 'blk'), as said below
- coupling_first: bfloat16 [6144, 2048], P('leaf', 'blk'), may hold values from -0.109375 to 0.109375
- structure_first: int32 [6144], P('leaf'), may hold values from 0 to 4095, as said below
- noise_second: float32 [2048, 2048], P('blk', 'leaf'), may hold values from -6 to 6
- block_second: bfloat16 [8192, 2048], P('leaf', 'blk'), as said below
- coupling_second: bfloat16 [12288, 2048], P('leaf', 'blk'), may hold values from -0.109375 to 0.109375
- structure_second: int32 [12288], P('leaf'), may hold values from 0 to 6143, as said below
- noise_third: float32 [1024, 4096], P('blk', 'leaf'), may hold values from -6 to 6
- block_third: bfloat16 [8192, 1024], P('leaf', 'blk'), as said below
- coupling_third: bfloat16 [24576, 1024], P('leaf', 'blk'), may hold values from -0.109375 to 0.109375
- structure_third: int32 [24576], P('leaf'), may hold values from 0 to 8191, as said below
Outputs:
- solved_root: bfloat16 [4096, 512], P(('leaf', 'blk'))
- solved_first: bfloat16 [4096, 512], P(('leaf', 'blk'))
- solved_second: bfloat16 [8192, 512], P(('leaf', 'blk'))
- solved_third: bfloat16 [8192, 512], P(('leaf', 'blk'))
Inputs may be any that keep to these rules, and one draw needn't show every extreme that they name: `structure_first`: for each first-level supernode, its 3072 entries are distinct, ascending, and include 0 and 4095. `structure_second`: for each second-level supernode, its 3072 entries are distinct, ascending, and include 0 and 6143. `structure_third`: for each third-level supernode, its 3072 entries are distinct, ascending, and include 0 and 8191. `block_root`: tiles above the diagonal tiles are zero; diagonal tiles are lower triangular with positive diagonals. `block_first`: in each supernode's square block, tiles above the diagonal tiles are zero; diagonal tiles are lower triangular with positive diagonals. `block_second`: in each supernode's square block, tiles above the diagonal tiles are zero; diagonal tiles are lower triangular with positive diagonals. `block_third`: in each supernode's square block, tiles above the diagonal tiles are zero; diagonal tiles are lower triangular with positive diagonals.
All inputs are finite; a program needn't handle non-finite values.
Results may differ from a plain program's by a relative error of at most 0.012.
Values may be sent and summed in bfloat16 or wider, within the bound.
No kernel may reach another device: no remote copies, remote signals or barrier semaphores. Data moves between devices by JAX's collectives and lax.ppermute only.
A program may use at most 128 MiB of HBM per device.

v0:
```python
import jax
import jax.numpy as jnp
from jax import lax
from jax.sharding import PartitionSpec as P


def partner(block, axis, bit):
    count = lax.axis_size(axis)
    route = []
    for low in range(count):
        high = low | 1 << bit
        if high != low and high < count:
            route += [(low, high), (high, low)]
    return lax.ppermute(block, axis, route)


def broadcast(array, axis, root):
    mine = lax.axis_index(axis) == root
    return lax.psum(jnp.where(mine, array, jnp.zeros_like(array)), axis)


def transposed_product(left, right):
    return lax.dot_general(
        left, right, (((0,), (0,)), ((), ())), preferred_element_type=jnp.float32
    )


def gather_group(local_rows, group_index, level_bits):
    entire = lax.all_gather(local_rows, "leaf", axis=0, tiled=True)
    span_rows = local_rows.shape[0] << level_bits
    return lax.dynamic_slice_in_dim(entire, group_index * span_rows, span_rows, 0)


def sum_in_group(partial_value, level_bits):
    total = partial_value
    for bit_number in range(level_bits):
        total = total + partner(total, "leaf", bit_number)
    return total


def solve_chain(column_tile, residual, blk_index, blk_count, tile_rows):
    inverse = lax.dynamic_slice_in_dim(column_tile, blk_index * tile_rows, tile_rows, 0)
    accumulated = jnp.zeros(residual.shape, jnp.float32)
    solutions = [None] * blk_count

    def own_solve(right_side):
        return transposed_product(inverse, right_side).astype(jnp.bfloat16)

    def no_solve(right_side):
        return jnp.zeros(right_side.shape, jnp.bfloat16)

    for target in reversed(range(blk_count)):
        right_side = (residual - accumulated).astype(jnp.bfloat16)
        own_tile = lax.cond(blk_index == target, own_solve, no_solve, right_side)
        solved_tile = broadcast(own_tile, "blk", target)
        solutions[target] = solved_tile
        if target > 0:
            tile_block = column_tile[target * tile_rows : (target + 1) * tile_rows]
            contribution = transposed_product(tile_block, solved_tile)
            accumulated = accumulated + jnp.where(blk_index < target, contribution, 0.0)
    return jnp.concatenate(solutions, 0)


def local(
    noise_root,
    block_root,
    noise_first,
    block_first,
    coupling_first,
    structure_first,
    noise_second,
    block_second,
    coupling_second,
    structure_second,
    noise_third,
    block_third,
    coupling_third,
    structure_third,
):
    leaf_index = lax.axis_index("leaf")
    blk_index = lax.axis_index("blk")
    leaf_count = lax.axis_size("leaf")
    blk_count = lax.axis_size("blk")
    levels_data = [
        (noise_root, block_root, None, None),
        (noise_first, block_first, coupling_first, structure_first),
        (noise_second, block_second, coupling_second, structure_second),
        (noise_third, block_third, coupling_third, structure_third),
    ]
    solved = []
    outputs = []
    for level_number, (noise, local_rows, coupling, structure) in enumerate(levels_data):
        group_size = leaf_count >> level_number
        level_bits = group_size.bit_length() - 1
        group_index = leaf_index // group_size
        member_index = leaf_index % group_size
        sep_rows = local_rows.shape[0] * group_size
        tile_rows = local_rows.shape[1]
        column_tile = gather_group(local_rows, group_index, level_bits)
        if level_number == 0:
            residual = noise
        else:
            ancestors = jnp.concatenate(solved, 0)
            picked = jnp.take(ancestors, structure, axis=0)
            partial_value = -transposed_product(coupling, picked)
            columns_each = noise.shape[1]
            noise_full = lax.dynamic_update_slice(
                jnp.zeros(partial_value.shape, jnp.float32), noise, (0, member_index * columns_each)
            )
            residual = sum_in_group(partial_value + noise_full, level_bits)
        supernode = solve_chain(column_tile, residual, blk_index, blk_count, tile_rows)
        solved.append(supernode)
        out_rows = sep_rows // (group_size * blk_count)
        start_row = member_index * (sep_rows // group_size) + blk_index * out_rows
        outputs.append(lax.dynamic_slice_in_dim(supernode, start_row, out_rows, 0))
    return (outputs[0], outputs[1], outputs[2], outputs[3])


def solution(mesh):
    in_specs = (
        P("blk", None),
        P("leaf", "blk"),
        P("blk", "leaf"),
        P("leaf", "blk"),
        P("leaf", "blk"),
        P("leaf"),
        P("blk", "leaf"),
        P("leaf", "blk"),
        P("leaf", "blk"),
        P("leaf"),
        P("blk", "leaf"),
        P("leaf", "blk"),
        P("leaf", "blk"),
        P("leaf"),
    )
    out_specs = (
        P(("leaf", "blk"), None),
        P(("leaf", "blk"), None),
        P(("leaf", "blk"), None),
        P(("leaf", "blk"), None),
    )
    return jax.shard_map(local, mesh=mesh, in_specs=in_specs, out_specs=out_specs, check_vma=False)
```

profile of v0, /device:TPU:1, one launch (start us, length us, event | category | flops | bytes accessed | tf_op | source)
XLA Modules:
  0.0 1534.2 jit_solution(11518332723813780028)
XLA Ops:
  10.7 192.3 %all-gather.5.cloned.1.call-done = bf16[4096,1024]{1,0:T(8,128)(2,1)} async-done(((bf16[128,1024]{1,0:T(8,128)(2,1)}), bf16[4096,1024]{1,0:T(8,128)(2,1)}) %all-gather.5.cloned.1.call-update) | async-done | bytes 8388624 | tf_op jit(solution)/shard_map/all_gather | solution.py:29
  209.9 43.1 %all-reduce.17.cloned.1.call-done = bf16[1024,512]{1,0:T(8,128)(2,1)} async-done(((bf16[1024,512]{1,0:T(8,128)(2,1)}), bf16[1024,512]{1,0:T(8,128)(2,1)}) %all-reduce.17.cloned.1.call-update) | async-done | bytes 1048592 | tf_op jit(solution)/shard_map/psum | solution.py:19
  253.0 5.5 fusion.8
  259.7 48.3 %all-reduce.19.cloned.1.call-done = bf16[1024,512]{1,0:T(8,128)(2,1)} async-done(((bf16[1024,512]{1,0:T(8,128)(2,1)}), bf16[1024,512]{1,0:T(8,128)(2,1)}) %all-reduce.19.cloned.1.call-update) | async-done | bytes 1048592 | tf_op jit(solution)/shard_map/psum | solution.py:19
  308.0 5.5 subtract_convert_fusion
  317.9 44.1 %all-reduce.21.cloned.1.call-done = bf16[1024,512]{1,0:T(8,128)(2,1)} async-done(((bf16[1024,512]{1,0:T(8,128)(2,1)}), bf16[1024,512]{1,0:T(8,128)(2,1)}) %all-reduce.21.cloned.1.call-update) | async-done | bytes 1048592 | tf_op jit(solution)/shard_map/psum | solution.py:19
  367.9 46.1 %all-reduce.23.cloned.1.call-done = bf16[1024,512]{1,0:T(8,128)(2,1)} async-done(((bf16[1024,512]{1,0:T(8,128)(2,1)}), bf16[1024,512]{1,0:T(8,128)(2,1)}) %all-reduce.23.cloned.1.call-update) | async-done | bytes 1048592 | tf_op jit(solution)/shard_map/psum | solution.py:19
  427.6 44.2 %collective-permute-done = f32[512,512]{0,1:T(8,128)S(1)} collective-permute-done((f32[512,512]{0,1:T(8,128)S(1)}, f32[512,512]{0,1:T(8,128)S(1)}, u32[]{:S(2)}, u32[]{:S(2)}) %collective-permute-start) | collective-permute-done | bytes 1048608 | tf_op jit(solution)/shard_map/ppermute | solution.py:14
  472.1 4.2 collective-permute-start.1
  476.3 31.1 %collective-permute-done.1 = f32[512,512]{0,1:T(8,128)S(1)} collective-permute-done((f32[512,512]{0,1:T(8,128)S(1)}, f32[512,512]{0,1:T(8,128)S(1)}, u32[]{:S(2)}, u32[]{:S(2)}) %collective-permute-start.1) | collective-permute-done | bytes 1048608 | tf_op jit(solution)/shard_map/ppermute | solution.py:14
  511.3 33.4 %collective-permute-done.2 = f32[512,512]{0,1:T(8,128)S(1)} collective-permute-done((f32[512,512]{0,1:T(8,128)S(1)}, f32[512,512]{0,1:T(8,128)S(1)}, u32[]{:S(2)}, u32[]{:S(2)}) %collective-permute-start.2) | collective-permute-done | bytes 1048608 | tf_op jit(solution)/shard_map/ppermute | solution.py:14
  547.6 25.0 %all-gather.7.cloned.1.call-done = bf16[4096,512]{1,0:T(8,128)(2,1)} async-done(((bf16[128,512]{1,0:T(8,128)(2,1)}), bf16[4096,512]{1,0:T(8,128)(2,1)}) %all-gather.7.cloned.1.call-update) | async-done | bytes 4194320 | tf_op jit(solution)/shard_map/all_gather | solution.py:29
  576.9 56.2 %all-reduce.25.cloned.1.call-done = bf16[512,512]{1,0:T(8,128)(2,1)} async-done(((bf16[512,512]{1,0:T(8,128)(2,1)}), bf16[512,512]{1,0:T(8,128)(2,1)}) %all-reduce.25.cloned.1.call-update) | async-done | bytes 524304 | tf_op jit(solution)/shard_map/psum | solution.py:19
  636.5 43.0 %all-reduce.27.cloned.1.call-done = bf16[512,512]{1,0:T(8,128)(2,1)} async-done(((bf16[512,512]{1,0:T(8,128)(2,1)}), bf16[512,512]{1,0:T(8,128)(2,1)}) %all-reduce.27.cloned.1.call-update) | async-done | bytes 524304 | tf_op jit(solution)/shard_map/psum | solution.py:19
  683.6 41.2 %all-reduce.29.cloned.1.call-done = bf16[512,512]{1,0:T(8,128)(2,1)} async-done(((bf16[512,512]{1,0:T(8,128)(2,1)}), bf16[512,512]{1,0:T(8,128)(2,1)}) %all-reduce.29.cloned.1.call-update) | async-done | bytes 524304 | tf_op jit(solution)/shard_map/psum | solution.py:19
  729.5 41.8 %all-reduce.31.cloned.1.call-done = bf16[512,512]{1,0:T(8,128)(2,1)} async-done(((bf16[512,512]{1,0:T(8,128)(2,1)}), bf16[512,512]{1,0:T(8,128)(2,1)}) %all-reduce.31.cloned.1.call-update) | async-done | bytes 524304 | tf_op jit(solution)/shard_map/psum | solution.py:19
  776.7 5.7 gather_fusion.1
  783.4 47.2 %collective-permute-done.4 = f32[512,512]{0,1:T(8,128)S(1)} collective-permute-done((f32[512,512]{0,1:T(8,128)S(1)}, f32[512,512]{0,1:T(8,128)S(1)}, u32[]{:S(2)}, u32[]{:S(2)}) %collective-permute-start.4) | collective-permute-done | bytes 1048608 | tf_op jit(solution)/shard_map/ppermute | solution.py:14
  832.1 43.3 %collective-permute-done.5 = f32[512,512]{0,1:T(8,128)S(1)} collective-permute-done((f32[512,512]{0,1:T(8,128)S(1)}, f32[512,512]{0,1:T(8,128)S(1)}, u32[]{:S(2)}, u32[]{:S(2)}) %collective-permute-start.5) | collective-permute-done | bytes 1048608 | tf_op jit(solution)/shard_map/ppermute | solution.py:14
  878.6 102.6 %all-gather.9.cloned.1.call-done = bf16[8192,512]{1,0:T(8,128)(2,1)} async-done(((bf16[256,512]{1,0:T(8,128)(2,1)}), bf16[8192,512]{1,0:T(8,128)(2,1)}) %all-gather.9.cloned.1.call-update) | async-done | bytes 8388624 | tf_op jit(solution)/shard_map/all_gather | solution.py:29
  985.9 46.8 %all-reduce.33.cloned.1.call-done = bf16[512,512]{1,0:T(8,128)(2,1)} async-done(((bf16[512,512]{1,0:T(8,128)(2,1)}), bf16[512,512]{1,0:T(8,128)(2,1)}) %all-reduce.33.cloned.1.call-update) | async-done | bytes 524304 | tf_op jit(solution)/shard_map/psum | solution.py:19
  1037.2 43.1 %all-reduce.35.cloned.1.call-done = bf16[512,512]{1,0:T(8,128)(2,1)} async-done(((bf16[512,512]{1,0:T(8,128)(2,1)}), bf16[512,512]{1,0:T(8,128)(2,1)}) %all-reduce.35.cloned.1.call-update) | async-done | bytes 524304 | tf_op jit(solution)/shard_map/psum | solution.py:19
  1086.6 41.0 %all-reduce.37.cloned.1.call-done = bf16[512,512]{1,0:T(8,128)(2,1)} async-done(((bf16[512,512]{1,0:T(8,128)(2,1)}), bf16[512,512]{1,0:T(8,128)(2,1)}) %all-reduce.37.cloned.1.call-update) | async-done | bytes 524304 | tf_op jit(solution)/shard_map/psum | solution.py:19
  1134.6 41.3 %all-reduce.39.cloned.1.call-done = bf16[512,512]{1,0:T(8,128)(2,1)} async-done(((bf16[512,512]{1,0:T(8,128)(2,1)}), bf16[512,512]{1,0:T(8,128)(2,1)}) %all-reduce.39.cloned.1.call-update) | async-done | bytes 524304 | tf_op jit(solution)/shard_map/psum | solution.py:19
  1180.3 7.2 gather_fusion.2
  1189.6 21.2 %collective-permute-done.7 = f32[256,512]{0,1:T(8,128)S(1)} collective-permute-done((f32[256,512]{0,1:T(8,128)S(1)}, f32[256,512]{0,1:T(8,128)S(1)}, u32[]{:S(2)}, u32[]{:S(2)}) %collective-permute-start.7) | collective-permute-done | bytes 524320 | tf_op jit(solution)/shard_map/ppermute | solution.py:14
  1210.8 4.5 collective-permute-start.8
  1215.3 113.1 %all-gather.11.cloned.1.call-done = bf16[8192,256]{1,0:T(8,128)(2,1)} async-done(((bf16[256,256]{1,0:T(8,128)(2,1)}), bf16[8192,256]{1,0:T(8,128)(2,1)}) %all-gather.11.cloned.1.call-update) | async-done | bytes 4194320 | tf_op jit(solution)/shard_map/all_gather | solution.py:29
  1332.7 56.4 %all-reduce.41.cloned.1.call-done = bf16[256,512]{1,0:T(8,128)(2,1)} async-done(((bf16[256,512]{1,0:T(8,128)(2,1)}), bf16[256,512]{1,0:T(8,128)(2,1)}) %all-reduce.41.cloned.1.call-update) | async-done | bytes 262160 | tf_op jit(solution)/shard_map/psum | solution.py:19
  1392.7 42.2 %all-reduce.43.cloned.1.call-done = bf16[256,512]{1,0:T(8,128)(2,1)} async-done(((bf16[256,512]{1,0:T(8,128)(2,1)}), bf16[256,512]{1,0:T(8,128)(2,1)}) %all-reduce.43.cloned.1.call-update) | async-done | bytes 262160 | tf_op jit(solution)/shard_map/psum | solution.py:19
  1441.0 39.4 %all-reduce.45.cloned.1.call-done = bf16[256,512]{1,0:T(8,128)(2,1)} async-done(((bf16[256,512]{1,0:T(8,128)(2,1)}), bf16[256,512]{1,0:T(8,128)(2,1)}) %all-reduce.45.cloned.1.call-update) | async-done | bytes 262160 | tf_op jit(solution)/shard_map/psum | solution.py:19
  1488.4 37.4 %all-reduce.47.cloned.1.call-done = bf16[256,512]{1,0:T(8,128)(2,1)} async-done(((bf16[256,512]{1,0:T(8,128)(2,1)}), bf16[256,512]{1,0:T(8,128)(2,1)}) %all-reduce.47.cloned.1.call-update) | async-done | bytes 262160 | tf_op jit(solution)/shard_map/psum | solution.py:19
  (203 shorter events, 134.1 us)
Async XLA Ops:
  7.2 775.2 %copy-start = (bf16[384,512]{1,0:T(8,128)(2,1)S(1)}, bf16[384,512]{1,0:T(8,128)(2,1)}, u32[]{:S(2)}) copy-start(bf16[384,512]{1,0:T(8,128)(2,1)} %param.54) | copy-start | bytes 1179652
  7.2 195.8 %all-gather.5.cloned.1.call-start = ((), (), s32[]{:S(2)}) async-start(), calls=%async_computation | async-start | bytes 8650752 | tf_op jit(solution)/shard_map/all_gather | solution.py:29
  7.9 245.1 %all-reduce.17.cloned.1.call-start = ((), (), s32[]{:S(2)}) async-start(), calls=%async_computation.1 | async-start | bytes 2097152 | tf_op jit(solution)/shard_map/psum | solution.py:19
  207.2 100.8 %all-reduce.19.cloned.1.call-start = ((), (), s32[]{:S(2)}) async-start(), calls=%async_computation.2 | async-start | bytes 2097152 | tf_op jit(solution)/shard_map/psum | solution.py:19
  259.6 102.3 %all-reduce.21.cloned.1.call-start = ((), (), s32[]{:S(2)}) async-start(), calls=%async_computation.3 | async-start | bytes 2097152 | tf_op jit(solution)/shard_map/psum | solution.py:19
  317.8 96.1 %all-reduce.23.cloned.1.call-start = ((), (), s32[]{:S(2)}) async-start(), calls=%async_computation.4 | async-start | bytes 2097152 | tf_op jit(solution)/shard_map/psum | solution.py:19
  367.0 205.6 %all-gather.7.cloned.1.call-start = ((), (), s32[]{:S(2)}) async-start(), calls=%async_computation.5 | async-start | bytes 4325376 | tf_op jit(solution)/shard_map/all_gather | solution.py:29
  367.6 265.5 %all-reduce.25.cloned.1.call-start = ((), (), s32[]{:S(2)}) async-start(), calls=%async_computation.6 | async-start | bytes 1048576 | tf_op jit(solution)/shard_map/psum | solution.py:19
  427.3 44.6 %collective-permute-start = (f32[512,512]{0,1:T(8,128)S(1)}, f32[512,512]{0,1:T(8,128)S(1)}, u32[]{:S(2)}, u32[]{:S(2)}) collective-permute-start(f32[512,512]{0,1:T(8,128)S(1)} %fusion.51), channel_id=1, source_target_pairs={{0,4},{4,0},{8,12},{12,8},{16,20},{20,16},{24,28},{28,24},{32,36},... | collective-permute-start | bytes 3145736 | tf_op jit(solution)/shard_map/ppermute | solution.py:14
  472.1 35.3 %collective-permute-start.1 = (f32[512,512]{0,1:T(8,128)S(1)}, f32[512,512]{0,1:T(8,128)S(1)}, u32[]{:S(2)}, u32[]{:S(2)}) collective-permute-start(f32[512,512]{0,1:T(8,128)S(1)} %add.208), channel_id=1, source_target_pairs={{0,8},{8,0},{4,12},{12,4},{16,24},{24,16},{20,28},{28,20},{32,40},... | collective-permute-start | bytes 3145736 | tf_op jit(solution)/shard_map/ppermute | solution.py:14
  507.6 37.1 %collective-permute-start.2 = (f32[512,512]{0,1:T(8,128)S(1)}, f32[512,512]{0,1:T(8,128)S(1)}, u32[]{:S(2)}, u32[]{:S(2)}) collective-permute-start(f32[512,512]{0,1:T(8,128)S(1)} %add.209), channel_id=1, source_target_pairs={{0,16},{16,0},{4,20},{20,4},{8,24},{24,8},{12,28},{28,12},{32,48},... | collective-permute-start | bytes 3145736 | tf_op jit(solution)/shard_map/ppermute | solution.py:14
  544.9 29.6 %collective-permute-start.3 = (f32[512,512]{0,1:T(8,128)S(1)}, f32[512,512]{0,1:T(8,128)}, u32[]{:S(2)}, u32[]{:S(2)}) collective-permute-start(f32[512,512]{0,1:T(8,128)S(1)} %add.210), channel_id=1, source_target_pairs={{0,32},{32,0},{4,36},{36,4},{8,40},{40,8},{12,44},{44,12},{16,48},... | collective-permute-start | bytes 3145736 | tf_op jit(solution)/shard_map/ppermute | solution.py:14
  576.8 102.6 %all-reduce.27.cloned.1.call-start = ((), (), s32[]{:S(2)}) async-start(), calls=%async_computation.7 | async-start | bytes 1048576 | tf_op jit(solution)/shard_map/psum | solution.py:19
  636.5 88.4 %all-reduce.29.cloned.1.call-start = ((), (), s32[]{:S(2)}) async-start(), calls=%async_computation.8 | async-start | bytes 1048576 | tf_op jit(solution)/shard_map/psum | solution.py:19
  683.6 87.7 %all-reduce.31.cloned.1.call-start = ((), (), s32[]{:S(2)}) async-start(), calls=%async_computation.9 | async-start | bytes 1048576 | tf_op jit(solution)/shard_map/psum | solution.py:19
  728.6 252.5 %all-gather.9.cloned.1.call-start = ((), (), s32[]{:S(2)}) async-start(), calls=%async_computation.10 | async-start | bytes 8650752 | tf_op jit(solution)/shard_map/all_gather | solution.py:29
  729.4 303.4 %all-reduce.33.cloned.1.call-start = ((), (), s32[]{:S(2)}) async-start(), calls=%async_computation.11 | async-start | bytes 1048576 | tf_op jit(solution)/shard_map/psum | solution.py:19
  783.1 47.6 %collective-permute-start.4 = (f32[512,512]{0,1:T(8,128)S(1)}, f32[512,512]{0,1:T(8,128)S(1)}, u32[]{:S(2)}, u32[]{:S(2)}) collective-permute-start(f32[512,512]{0,1:T(8,128)S(1)} %fusion.43), channel_id=1, source_target_pairs={{0,4},{4,0},{8,12},{12,8},{16,20},{20,16},{24,28},{28,24},{32,36},... | collective-permute-start | bytes 3145736 | tf_op jit(solution)/shard_map/ppermute | solution.py:14
  830.9 44.6 %collective-permute-start.5 = (f32[512,512]{0,1:T(8,128)S(1)}, f32[512,512]{0,1:T(8,128)S(1)}, u32[]{:S(2)}, u32[]{:S(2)}) collective-permute-start(f32[512,512]{0,1:T(8,128)S(1)} %add.222), channel_id=1, source_target_pairs={{0,8},{8,0},{4,12},{12,4},{16,24},{24,16},{20,28},{28,20},{32,40},... | collective-permute-start | bytes 3145736 | tf_op jit(solution)/shard_map/ppermute | solution.py:14
  875.7 106.7 %copy-start.11 = (f32[512,512]{0,1:T(8,128)}, f32[512,512]{0,1:T(8,128)S(1)}, u32[]{:S(2)}) copy-start(f32[512,512]{0,1:T(8,128)S(1)} %add.223) | copy-start | bytes 3145732
  875.7 106.7 %collective-permute-start.6 = (f32[512,512]{0,1:T(8,128)S(1)}, f32[512,512]{0,1:T(8,128)}, u32[]{:S(2)}, u32[]{:S(2)}) collective-permute-start(f32[512,512]{0,1:T(8,128)S(1)} %add.223), channel_id=1, source_target_pairs={{0,16},{16,0},{4,20},{20,4},{8,24},{24,8},{12,28},{28,12},{32,48},... | collective-permute-start | bytes 3145736 | tf_op jit(solution)/shard_map/ppermute | solution.py:14
  985.9 94.5 %all-reduce.35.cloned.1.call-start = ((), (), s32[]{:S(2)}) async-start(), calls=%async_computation.12 | async-start | bytes 1048576 | tf_op jit(solution)/shard_map/psum | solution.py:19
  1037.2 90.5 %all-reduce.37.cloned.1.call-start = ((), (), s32[]{:S(2)}) async-start(), calls=%async_computation.13 | async-start | bytes 1048576 | tf_op jit(solution)/shard_map/psum | solution.py:19
  1086.6 89.3 %all-reduce.39.cloned.1.call-start = ((), (), s32[]{:S(2)}) async-start(), calls=%async_computation.14 | async-start | bytes 1048576 | tf_op jit(solution)/shard_map/psum | solution.py:19
  1132.2 196.2 %all-gather.11.cloned.1.call-start = ((), (), s32[]{:S(2)}) async-start(), calls=%async_computation.15 | async-start | bytes 4325376 | tf_op jit(solution)/shard_map/all_gather | solution.py:29
  1132.8 256.2 %all-reduce.41.cloned.1.call-start = ((), (), s32[]{:S(2)}) async-start(), calls=%async_computation.16 | async-start | bytes 524288 | tf_op jit(solution)/shard_map/psum | solution.py:19
  1189.2 21.5 %collective-permute-start.7 = (f32[256,512]{0,1:T(8,128)S(1)}, f32[256,512]{0,1:T(8,128)S(1)}, u32[]{:S(2)}, u32[]{:S(2)}) collective-permute-start(f32[256,512]{0,1:T(8,128)S(1)} %fusion.42), channel_id=1, source_target_pairs={{0,4},{4,0},{8,12},{12,8},{16,20},{20,16},{24,28},{28,24},{32,36},... | collective-permute-start | bytes 1572872 | tf_op jit(solution)/shard_map/ppermute | solution.py:14
  1210.8 119.2 %collective-permute-start.8 = (f32[256,512]{0,1:T(8,128)S(1)}, f32[256,512]{0,1:T(8,128)}, u32[]{:S(2)}, u32[]{:S(2)}) collective-permute-start(f32[256,512]{0,1:T(8,128)S(1)} %add.236), channel_id=1, source_target_pairs={{0,8},{8,0},{4,12},{12,4},{16,24},{24,16},{20,28},{28,20},{32,40},... | collective-permute-start | bytes 1572872 | tf_op jit(solution)/shard_map/ppermute | solution.py:14
  1332.6 102.2 %all-reduce.43.cloned.1.call-start = ((), (), s32[]{:S(2)}) async-start(), calls=%async_computation.17 | async-start | bytes 524288 | tf_op jit(solution)/shard_map/psum | solution.py:19
  1391.9 93.6 %copy-start.7 = (bf16[512,512]{1,0:T(8,128)(2,1)S(1)}, bf16[512,512]{1,0:T(8,128)(2,1)}, u32[]{:S(2)}) copy-start(bf16[512,512]{1,0:T(8,128)(2,1)} %all-reduce.29.cloned.1.call-done) | copy-start | bytes 1572868
  1392.6 87.8 %all-reduce.45.cloned.1.call-start = ((), (), s32[]{:S(2)}) async-start(), calls=%async_computation.18 | async-start | bytes 524288 | tf_op jit(solution)/shard_map/psum | solution.py:19
  1440.9 84.9 %all-reduce.47.cloned.1.call-start = ((), (), s32[]{:S(2)}) async-start(), calls=%async_computation.19 | async-start | bytes 524288 | tf_op jit(solution)/shard_map/psum | solution.py:19
  (19 other events, 578.8 us)
Sparse Core Ops, SparseCore 0:
  9.7 193.2 all-gather.4
  207.3 45.6 all-reduce.16
  259.8 48.2 all-reduce.18
  317.9 44.0 all-reduce.20
  367.1 46.7 all-reduce.22
  415.4 157.1 all-gather.6
  576.9 56.0 all-reduce.24
  636.6 42.8 all-reduce.26
  683.7 41.0 all-reduce.28
  728.8 42.4 all-reduce.30
  772.9 208.1 all-gather.8
  986.0 46.7 all-reduce.32
  1037.3 42.9 all-reduce.34
  1086.7 40.8 all-reduce.36
  1132.3 43.4 all-reduce.38
  1177.4 150.9 all-gather.10
  1332.7 56.2 all-reduce.40
  1392.7 42.0 all-reduce.42
  1441.0 39.3 all-reduce.44
  1484.2 41.5 all-reduce.46
where the time goes:
time: 1540 us; the launch traced here: 1530 us
  waiting for transfers between devices  1370 us (89%)
  local copies, waits for them, and re-layouts  53.6 us (3%)
  matrix products  46.8 us (3%)
  other arithmetic  29.5 us (2%)
  starting transfers between devices  21.4 us (1%)
    psum x16, waiting for transfers between devices, broadcast(): return lax.psum(jnp.where(mine, array, jnp.zeros_like(array)), axis)  711 us
    all_gather x4, waiting for transfers between devices, gather_group(): entire = lax.all_gather(local_rows, 'leaf', axis=0, tiled=True)  433 us
    ppermute x9, waiting for transfers between devices, partner(): return lax.ppermute(block, axis, route)  221 us
    dot_general x19, matrix products, transposed_product(): lax.dot_general(left, right, (((0,), (0,)), ((), ())), preferred_element_...  46.8 us
  transfers between devices with their start and end apart: 29, of which 27 were waited for; matrix products, arithmetic and copies ran while one was open for 4% of the time, Pallas kernels for 0%

commit v1 on v0

--- a/solution.py
+++ b/solution.py
@@ -16,7 +16,7 @@
 
 def broadcast(array, axis, root):
     mine = lax.axis_index(axis) == root
-    return lax.psum(jnp.where(mine, array, jnp.zeros_like(array)), axis)
+    return jnp.sum(lax.all_gather(jnp.where(mine, array, jnp.zeros_like(array)), axis), axis=0)
 
 
 def transposed_product(left, right):

time: 1540 us -> 1360 us (0.88)
  waiting for transfers between devices: 1370 us -> 1130 us
  other arithmetic: 29.5 us -> 74.9 us
    psum x16 -> x0, waiting for transfers between devices: 711 us -> none  [broadcast(): return lax.psum(jnp.where(mine, array, jnp.zeros_like(array)), axis)]
    all_gather x0 -> x16, waiting for transfers between devices: none -> 476 us  [broadcast(): lax.all_gather(jnp.where(mine, array, jnp.zeros_like(array)), axis)]
    reduce_sum x0 -> x16, other arithmetic: none -> 40.7 us  [broadcast(): jnp.sum(lax.all_gather(jnp.where(mine, array, jnp.zeros_like(array)), axi...]
  transfers between devices with their start and end apart: 29 -> 29, of which waited for: 27 -> 26; matrix products, arithmetic and copies ran while one was open for 4% -> 5% of each run, Pallas kernels for 0% -> 0%
where the time goes in v1:
time: 1360 us; the launch traced here: 1350 us
  waiting for transfers between devices  1130 us (83%)
  other arithmetic  74.9 us (6%)
  matrix products  54.7 us (4%)
  local copies, waits for them, and re-layouts  52.1 us (4%)
  starting transfers between devices  21 us (2%)
  between operations  15.2 us (1%)
    all_gather x16, waiting for transfers between devices, broadcast(): lax.all_gather(jnp.where(mine, array, jnp.zeros_like(array)), axis)  476 us
    all_gather x4, waiting for transfers between devices, gather_group(): entire = lax.all_gather(local_rows, 'leaf', axis=0, tiled=True)  431 us
    ppermute x9, waiting for transfers between devices, partner(): return lax.ppermute(block, axis, route)  221 us
    dot_general x19, matrix products, transposed_product(): lax.dot_general(left, right, (((0,), (0,)), ((), ())), preferred_element_...  54.7 us
    reduce_sum x16, other arithmetic, broadcast(): jnp.sum(lax.all_gather(jnp.where(mine, array, jnp.zeros_like(array)), axi...  40.7 us
  transfers between devices with their start and end apart: 29, of which 26 were waited for; matrix products, arithmetic and copies ran while one was open for 5% of the time, Pallas kernels for 0%

profile of v1, /device:TPU:1, one launch (start us, length us, event | category | flops | bytes accessed | tf_op | source)
XLA Modules:
  0.0 1348.9 jit_solution(4347207541375134804)
XLA Ops:
  10.7 192.3 %all-gather.37.cloned.1.call-done = bf16[4096,1024]{1,0:T(8,128)(2,1)} async-done(((bf16[128,1024]{1,0:T(8,128)(2,1)}), bf16[4096,1024]{1,0:T(8,128)(2,1)}) %all-gather.37.cloned.1.call-update) | async-done | bytes 8388624 | tf_op jit(solution)/shard_map/all_gather | solution.py:29
  209.9 36.3 %all-gather.45.cloned.1.call-done = bf16[4096,512]{1,0:T(8,128)(2,1)} async-done(((bf16[1024,512]{1,0:T(8,128)(2,1)}), bf16[4096,512]{1,0:T(8,128)(2,1)}) %all-gather.45.cloned.1.call-update) | async-done | bytes 4194320 | tf_op jit(solution)/shard_map/all_gather | solution.py:19
  249.7 5.2 fusion.8
  256.1 40.9 %all-gather.47.cloned.1.call-done = bf16[4096,512]{1,0:T(8,128)(2,1)} async-done(((bf16[1024,512]{1,0:T(8,128)(2,1)}), bf16[4096,512]{1,0:T(8,128)(2,1)}) %all-gather.47.cloned.1.call-update) | async-done | bytes 4194320 | tf_op jit(solution)/shard_map/all_gather | solution.py:19
  300.5 5.8 subtract_convert_fusion
  310.6 37.4 %all-gather.49.cloned.1.call-done = bf16[4096,512]{1,0:T(8,128)(2,1)} async-done(((bf16[1024,512]{1,0:T(8,128)(2,1)}), bf16[4096,512]{1,0:T(8,128)(2,1)}) %all-gather.49.cloned.1.call-update) | async-done | bytes 4194320 | tf_op jit(solution)/shard_map/all_gather | solution.py:19
  351.5 5.5 fusion.7
  360.3 41.1 %all-gather.51.cloned.1.call-done = bf16[4096,512]{1,0:T(8,128)(2,1)} async-done(((bf16[1024,512]{1,0:T(8,128)(2,1)}), bf16[4096,512]{1,0:T(8,128)(2,1)}) %all-gather.51.cloned.1.call-update) | async-done | bytes 4194320 | tf_op jit(solution)/shard_map/all_gather | solution.py:19
  401.4 4.1 reduce_sum.195
  414.5 44.3 %collective-permute-done = f32[512,512]{0,1:T(8,128)S(1)} collective-permute-done((f32[512,512]{0,1:T(8,128)S(1)}, f32[512,512]{0,1:T(8,128)S(1)}, u32[]{:S(2)}, u32[]{:S(2)}) %collective-permute-start) | collective-permute-done | bytes 1048608 | tf_op jit(solution)/shard_map/ppermute | solution.py:14
  462.9 31.3 %collective-permute-done.1 = f32[512,512]{0,1:T(8,128)S(1)} collective-permute-done((f32[512,512]{0,1:T(8,128)S(1)}, f32[512,512]{0,1:T(8,128)S(1)}, u32[]{:S(2)}, u32[]{:S(2)}) %collective-permute-start.1) | collective-permute-done | bytes 1048608 | tf_op jit(solution)/shard_map/ppermute | solution.py:14
  498.6 32.8 %collective-permute-done.2 = f32[512,512]{0,1:T(8,128)S(1)} collective-permute-done((f32[512,512]{0,1:T(8,128)S(1)}, f32[512,512]{0,1:T(8,128)S(1)}, u32[]{:S(2)}, u32[]{:S(2)}) %collective-permute-start.2) | collective-permute-done | bytes 1048608 | tf_op jit(solution)/shard_map/ppermute | solution.py:14
  535.2 24.8 %all-gather.39.cloned.1.call-done = bf16[4096,512]{1,0:T(8,128)(2,1)} async-done(((bf16[128,512]{1,0:T(8,128)(2,1)}), bf16[4096,512]{1,0:T(8,128)(2,1)}) %all-gather.39.cloned.1.call-update) | async-done | bytes 4194320 | tf_op jit(solution)/shard_map/all_gather | solution.py:29
  564.8 40.3 %all-gather.53.cloned.1.call-done = bf16[2048,512]{1,0:T(8,128)(2,1)} async-done(((bf16[512,512]{1,0:T(8,128)(2,1)}), bf16[2048,512]{1,0:T(8,128)(2,1)}) %all-gather.53.cloned.1.call-update) | async-done | bytes 2097168 | tf_op jit(solution)/shard_map/all_gather | solution.py:19
  612.0 28.7 %all-gather.55.cloned.1.call-done = bf16[2048,512]{1,0:T(8,128)(2,1)} async-done(((bf16[512,512]{1,0:T(8,128)(2,1)}), bf16[2048,512]{1,0:T(8,128)(2,1)}) %all-gather.55.cloned.1.call-update) | async-done | bytes 2097168 | tf_op jit(solution)/shard_map/all_gather | solution.py:19
  650.3 25.5 %all-gather.57.cloned.1.call-done = bf16[2048,512]{1,0:T(8,128)(2,1)} async-done(((bf16[512,512]{1,0:T(8,128)(2,1)}), bf16[2048,512]{1,0:T(8,128)(2,1)}) %all-gather.57.cloned.1.call-update) | async-done | bytes 2097168 | tf_op jit(solution)/shard_map/all_gather | solution.py:19
  691.4 20.0 %all-gather.59.cloned.1.call-done = bf16[2048,512]{1,0:T(8,128)(2,1)} async-done(((bf16[512,512]{1,0:T(8,128)(2,1)}), bf16[2048,512]{1,0:T(8,128)(2,1)}) %all-gather.59.cloned.1.call-update) | async-done | bytes 2097168 | tf_op jit(solution)/shard_map/all_gather | solution.py:19
  717.9 5.7 gather_fusion.1
  724.6 47.2 %collective-permute-done.4 = f32[512,512]{0,1:T(8,128)S(1)} collective-permute-done((f32[512,512]{0,1:T(8,128)S(1)}, f32[512,512]{0,1:T(8,128)S(1)}, u32[]{:S(2)}, u32[]{:S(2)}) %collective-permute-start.4) | collective-permute-done | bytes 1048608 | tf_op jit(solution)/shard_map/ppermute | solution.py:14
  773.3 43.4 %collective-permute-done.5 = f32[512,512]{0,1:T(8,128)S(1)} collective-permute-done((f32[512,512]{0,1:T(8,128)S(1)}, f32[512,512]{0,1:T(8,128)S(1)}, u32[]{:S(2)}, u32[]{:S(2)}) %collective-permute-start.5) | collective-permute-done | bytes 1048608 | tf_op jit(solution)/shard_map/ppermute | solution.py:14
  819.2 102.1 %all-gather.41.cloned.1.call-done = bf16[8192,512]{1,0:T(8,128)(2,1)} async-done(((bf16[256,512]{1,0:T(8,128)(2,1)}), bf16[8192,512]{1,0:T(8,128)(2,1)}) %all-gather.41.cloned.1.call-update) | async-done | bytes 8388624 | tf_op jit(solution)/shard_map/all_gather | solution.py:29
  926.1 31.3 %all-gather.61.cloned.1.call-done = bf16[2048,512]{1,0:T(8,128)(2,1)} async-done(((bf16[512,512]{1,0:T(8,128)(2,1)}), bf16[2048,512]{1,0:T(8,128)(2,1)}) %all-gather.61.cloned.1.call-update) | async-done | bytes 2097168 | tf_op jit(solution)/shard_map/all_gather | solution.py:19
  964.3 28.7 %all-gather.63.cloned.1.call-done = bf16[2048,512]{1,0:T(8,128)(2,1)} async-done(((bf16[512,512]{1,0:T(8,128)(2,1)}), bf16[2048,512]{1,0:T(8,128)(2,1)}) %all-gather.63.cloned.1.call-update) | async-done | bytes 2097168 | tf_op jit(solution)/shard_map/all_gather | solution.py:19
  1002.6 25.5 %all-gather.65.cloned.1.call-done = bf16[2048,512]{1,0:T(8,128)(2,1)} async-done(((bf16[512,512]{1,0:T(8,128)(2,1)}), bf16[2048,512]{1,0:T(8,128)(2,1)}) %all-gather.65.cloned.1.call-update) | async-done | bytes 2097168 | tf_op jit(solution)/shard_map/all_gather | solution.py:19
  1038.1 25.7 %all-gather.67.cloned.1.call-done = bf16[2048,512]{1,0:T(8,128)(2,1)} async-done(((bf16[512,512]{1,0:T(8,128)(2,1)}), bf16[2048,512]{1,0:T(8,128)(2,1)}) %all-gather.67.cloned.1.call-update) | async-done | bytes 2097168 | tf_op jit(solution)/shard_map/all_gather | solution.py:19
  1069.4 7.8 gather_fusion.2
  1080.4 22.2 %collective-permute-done.7 = f32[256,512]{0,1:T(8,128)S(1)} collective-permute-done((f32[256,512]{0,1:T(8,128)S(1)}, f32[256,512]{0,1:T(8,128)S(1)}, u32[]{:S(2)}, u32[]{:S(2)}) %collective-permute-start.7) | collective-permute-done | bytes 524320 | tf_op jit(solution)/shard_map/ppermute | solution.py:14
  1106.1 111.3 %all-gather.43.cloned.1.call-done = bf16[8192,256]{1,0:T(8,128)(2,1)} async-done(((bf16[256,256]{1,0:T(8,128)(2,1)}), bf16[8192,256]{1,0:T(8,128)(2,1)}) %all-gather.43.cloned.1.call-update) | async-done | bytes 4194320 | tf_op jit(solution)/shard_map/all_gather | solution.py:29
  1221.7 36.0 %all-gather.69.cloned.1.call-done = bf16[1024,512]{1,0:T(8,128)(2,1)} async-done(((bf16[256,512]{1,0:T(8,128)(2,1)}), bf16[1024,512]{1,0:T(8,128)(2,1)}) %all-gather.69.cloned.1.call-update) | async-done | bytes 1048592 | tf_op jit(solution)/shard_map/all_gather | solution.py:19
  1262.3 21.6 %all-gather.71.cloned.1.call-done = bf16[1024,512]{1,0:T(8,128)(2,1)} async-done(((bf16[256,512]{1,0:T(8,128)(2,1)}), bf16[1024,512]{1,0:T(8,128)(2,1)}) %all-gather.71.cloned.1.call-update) | async-done | bytes 1048592 | tf_op jit(solution)/shard_map/all_gather | solution.py:19
  1292.2 19.6 %all-gather.73.cloned.1.call-done = bf16[1024,512]{1,0:T(8,128)(2,1)} async-done(((bf16[256,512]{1,0:T(8,128)(2,1)}), bf16[1024,512]{1,0:T(8,128)(2,1)}) %all-gather.73.cloned.1.call-update) | async-done | bytes 1048592 | tf_op jit(solution)/shard_map/all_gather | solution.py:19
  1322.0 17.6 %all-gather.75.cloned.1.call-done = bf16[1024,512]{1,0:T(8,128)(2,1)} async-done(((bf16[256,512]{1,0:T(8,128)(2,1)}), bf16[1024,512]{1,0:T(8,128)(2,1)}) %all-gather.75.cloned.1.call-update) | async-done | bytes 1048592 | tf_op jit(solution)/shard_map/all_gather | solution.py:19
  (224 shorter events, 188.5 us)
Async XLA Ops:
  7.2 716.4 %copy-start = (bf16[384,512]{1,0:T(8,128)(2,1)S(1)}, bf16[384,512]{1,0:T(8,128)(2,1)}, u32[]{:S(2)}) copy-start(bf16[384,512]{1,0:T(8,128)(2,1)} %param.54) | copy-start | bytes 1179652
  7.2 195.8 %all-gather.37.cloned.1.call-start = ((), (), s32[]{:S(2)}) async-start(), calls=%async_computation | async-start | bytes 8650752 | tf_op jit(solution)/shard_map/all_gather | solution.py:29
  7.9 238.3 %all-gather.45.cloned.1.call-start = ((), (), s32[]{:S(2)}) async-start(), calls=%async_computation.4 | async-start | bytes 5242880 | tf_op jit(solution)/shard_map/all_gather | solution.py:19
  207.2 89.8 %all-gather.47.cloned.1.call-start = ((), (), s32[]{:S(2)}) async-start(), calls=%async_computation.5 | async-start | bytes 5242880 | tf_op jit(solution)/shard_map/all_gather | solution.py:19
  249.7 155.9 %copy-start.1 = (bf16[1024,512]{1,0:T(8,128)(2,1)}, bf16[1024,512]{1,0:T(8,128)(2,1)S(1)}, u32[]{:S(2)}) copy-start(bf16[1024,512]{1,0:T(8,128)(2,1)S(1)} %reduce_sum.192) | copy-start | bytes 3145732
  256.1 91.9 %all-gather.49.cloned.1.call-start = ((), (), s32[]{:S(2)}) async-start(), calls=%async_computation.6 | async-start | bytes 5242880 | tf_op jit(solution)/shard_map/all_gather | solution.py:19
  310.6 90.9 %all-gather.51.cloned.1.call-start = ((), (), s32[]{:S(2)}) async-start(), calls=%async_computation.7 | async-start | bytes 5242880 | tf_op jit(solution)/shard_map/all_gather | solution.py:19
  359.6 200.4 %all-gather.39.cloned.1.call-start = ((), (), s32[]{:S(2)}) async-start(), calls=%async_computation.1 | async-start | bytes 4325376 | tf_op jit(solution)/shard_map/all_gather | solution.py:29
  360.2 244.9 %all-gather.53.cloned.1.call-start = ((), (), s32[]{:S(2)}) async-start(), calls=%async_computation.8 | async-start | bytes 2621440 | tf_op jit(solution)/shard_map/all_gather | solution.py:19
  414.1 44.7 %collective-permute-start = (f32[512,512]{0,1:T(8,128)S(1)}, f32[512,512]{0,1:T(8,128)S(1)}, u32[]{:S(2)}, u32[]{:S(2)}) collective-permute-start(f32[512,512]{0,1:T(8,128)S(1)} %fusion.51), channel_id=1, source_target_pairs={{0,4},{4,0},{8,12},{12,8},{16,20},{20,16},{24,28},{28,24},{32,36},... | collective-permute-start | bytes 3145736 | tf_op jit(solution)/shard_map/ppermute | solution.py:14
  459.0 35.3 %collective-permute-start.1 = (f32[512,512]{0,1:T(8,128)S(1)}, f32[512,512]{0,1:T(8,128)S(1)}, u32[]{:S(2)}, u32[]{:S(2)}) collective-permute-start(f32[512,512]{0,1:T(8,128)S(1)} %add.176), channel_id=1, source_target_pairs={{0,8},{8,0},{4,12},{12,4},{16,24},{24,16},{20,28},{28,20},{32,40},... | collective-permute-start | bytes 3145736 | tf_op jit(solution)/shard_map/ppermute | solution.py:14
  494.5 36.9 %collective-permute-start.2 = (f32[512,512]{0,1:T(8,128)S(1)}, f32[512,512]{0,1:T(8,128)S(1)}, u32[]{:S(2)}, u32[]{:S(2)}) collective-permute-start(f32[512,512]{0,1:T(8,128)S(1)} %add.177), channel_id=1, source_target_pairs={{0,16},{16,0},{4,20},{20,4},{8,24},{24,8},{12,28},{28,12},{32,48},... | collective-permute-start | bytes 3145736 | tf_op jit(solution)/shard_map/ppermute | solution.py:14
  531.6 29.6 %collective-permute-start.3 = (f32[512,512]{0,1:T(8,128)S(1)}, f32[512,512]{0,1:T(8,128)}, u32[]{:S(2)}, u32[]{:S(2)}) collective-permute-start(f32[512,512]{0,1:T(8,128)S(1)} %add.178), channel_id=1, source_target_pairs={{0,32},{32,0},{4,36},{36,4},{8,40},{40,8},{12,44},{44,12},{16,48},... | collective-permute-start | bytes 3145736 | tf_op jit(solution)/shard_map/ppermute | solution.py:14
  564.8 75.9 %all-gather.55.cloned.1.call-start = ((), (), s32[]{:S(2)}) async-start(), calls=%async_computation.9 | async-start | bytes 2621440 | tf_op jit(solution)/shard_map/all_gather | solution.py:19
  611.9 63.8 %all-gather.57.cloned.1.call-start = ((), (), s32[]{:S(2)}) async-start(), calls=%async_computation.10 | async-start | bytes 2621440 | tf_op jit(solution)/shard_map/all_gather | solution.py:19
  650.2 61.2 %all-gather.59.cloned.1.call-start = ((), (), s32[]{:S(2)}) async-start(), calls=%async_computation.11 | async-start | bytes 2621440 | tf_op jit(solution)/shard_map/all_gather | solution.py:19
  683.2 238.2 %all-gather.41.cloned.1.call-start = ((), (), s32[]{:S(2)}) async-start(), calls=%async_computation.2 | async-start | bytes 8650752 | tf_op jit(solution)/shard_map/all_gather | solution.py:29
  683.9 273.5 %all-gather.61.cloned.1.call-start = ((), (), s32[]{:S(2)}) async-start(), calls=%async_computation.12 | async-start | bytes 2621440 | tf_op jit(solution)/shard_map/all_gather | solution.py:19
  724.3 47.6 %collective-permute-start.4 = (f32[512,512]{0,1:T(8,128)S(1)}, f32[512,512]{0,1:T(8,128)S(1)}, u32[]{:S(2)}, u32[]{:S(2)}) collective-permute-start(f32[512,512]{0,1:T(8,128)S(1)} %fusion.43), channel_id=1, source_target_pairs={{0,4},{4,0},{8,12},{12,8},{16,20},{20,16},{24,28},{28,24},{32,36},... | collective-permute-start | bytes 3145736 | tf_op jit(solution)/shard_map/ppermute | solution.py:14
  772.0 44.7 %collective-permute-start.5 = (f32[512,512]{0,1:T(8,128)S(1)}, f32[512,512]{0,1:T(8,128)S(1)}, u32[]{:S(2)}, u32[]{:S(2)}) collective-permute-start(f32[512,512]{0,1:T(8,128)S(1)} %add.190), channel_id=1, source_target_pairs={{0,8},{8,0},{4,12},{12,4},{16,24},{24,16},{20,28},{28,20},{32,40},... | collective-permute-start | bytes 3145736 | tf_op jit(solution)/shard_map/ppermute | solution.py:14
  817.0 105.5 %copy-start.17 = (f32[512,512]{0,1:T(8,128)}, f32[512,512]{0,1:T(8,128)S(1)}, u32[]{:S(2)}) copy-start(f32[512,512]{0,1:T(8,128)S(1)} %add.191) | copy-start | bytes 3145732
  817.0 105.5 %collective-permute-start.6 = (f32[512,512]{0,1:T(8,128)S(1)}, f32[512,512]{0,1:T(8,128)}, u32[]{:S(2)}, u32[]{:S(2)}) collective-permute-start(f32[512,512]{0,1:T(8,128)S(1)} %add.191), channel_id=1, source_target_pairs={{0,16},{16,0},{4,20},{20,4},{8,24},{24,8},{12,28},{28,12},{32,48},... | collective-permute-start | bytes 3145736 | tf_op jit(solution)/shard_map/ppermute | solution.py:14
  926.1 67.0 %all-gather.63.cloned.1.call-start = ((), (), s32[]{:S(2)}) async-start(), calls=%async_computation.13 | async-start | bytes 2621440 | tf_op jit(solution)/shard_map/all_gather | solution.py:19
  964.3 63.8 %all-gather.65.cloned.1.call-start = ((), (), s32[]{:S(2)}) async-start(), calls=%async_computation.14 | async-start | bytes 2621440 | tf_op jit(solution)/shard_map/all_gather | solution.py:19
  1002.6 61.2 %all-gather.67.cloned.1.call-start = ((), (), s32[]{:S(2)}) async-start(), calls=%async_computation.15 | async-start | bytes 2621440 | tf_op jit(solution)/shard_map/all_gather | solution.py:19
  1035.5 182.0 %all-gather.43.cloned.1.call-start = ((), (), s32[]{:S(2)}) async-start(), calls=%async_computation.3 | async-start | bytes 4325376 | tf_op jit(solution)/shard_map/all_gather | solution.py:29
  1036.1 221.7 %all-gather.69.cloned.1.call-start = ((), (), s32[]{:S(2)}) async-start(), calls=%async_computation.16 | async-start | bytes 1310720 | tf_op jit(solution)/shard_map/all_gather | solution.py:19
  1080.0 22.6 %collective-permute-start.7 = (f32[256,512]{0,1:T(8,128)S(1)}, f32[256,512]{0,1:T(8,128)S(1)}, u32[]{:S(2)}, u32[]{:S(2)}) collective-permute-start(f32[256,512]{0,1:T(8,128)S(1)} %fusion.42), channel_id=1, source_target_pairs={{0,4},{4,0},{8,12},{12,8},{16,20},{20,16},{24,28},{28,24},{32,36},... | collective-permute-start | bytes 1572872 | tf_op jit(solution)/shard_map/ppermute | solution.py:14
  1102.7 116.4 %collective-permute-start.8 = (f32[256,512]{0,1:T(8,128)S(1)}, f32[256,512]{0,1:T(8,128)}, u32[]{:S(2)}, u32[]{:S(2)}) collective-permute-start(f32[256,512]{0,1:T(8,128)S(1)} %add.204), channel_id=1, source_target_pairs={{0,8},{8,0},{4,12},{12,4},{16,24},{24,16},{20,28},{28,20},{32,40},... | collective-permute-start | bytes 1572872 | tf_op jit(solution)/shard_map/ppermute | solution.py:14
  1221.7 62.1 %all-gather.71.cloned.1.call-start = ((), (), s32[]{:S(2)}) async-start(), calls=%async_computation.17 | async-start | bytes 1310720 | tf_op jit(solution)/shard_map/all_gather | solution.py:19
  1262.2 49.6 %all-gather.73.cloned.1.call-start = ((), (), s32[]{:S(2)}) async-start(), calls=%async_computation.18 | async-start | bytes 1310720 | tf_op jit(solution)/shard_map/all_gather | solution.py:19
  1292.1 47.5 %all-gather.75.cloned.1.call-start = ((), (), s32[]{:S(2)}) async-start(), calls=%async_computation.19 | async-start | bytes 1310720 | tf_op jit(solution)/shard_map/all_gather | solution.py:19
  (21 other events, 395.0 us)
Sparse Core Ops, SparseCore 0:
  9.7 193.2 all-gather.36
  207.4 38.7 all-gather.44
  256.2 40.7 all-gather.46
  310.7 37.2 all-gather.48
  359.7 41.6 all-gather.50
  402.9 157.0 all-gather.38
  564.9 40.1 all-gather.52
  612.1 28.5 all-gather.54
  650.3 25.3 all-gather.56
  683.3 28.0 all-gather.58
  713.1 208.2 all-gather.40
  926.2 31.1 all-gather.60
  964.4 28.5 all-gather.62
  1002.7 25.3 all-gather.64
  1035.6 28.1 all-gather.66
  1065.3 152.1 all-gather.42
  1221.8 35.9 all-gather.68
  1262.3 21.4 all-gather.70
  1292.3 19.4 all-gather.72
  1317.7 21.8 all-gather.74
